TPU v7x, 128 devices: a whole 4x4x4 slice. The times are simulated.
128 devices in a mesh: sp: 2 (over core), ep: 64 (over x, y, z).
Axes of the slice: x: 4, y: 4, z: 4, core: 2. Of those that a mesh axis runs over, the one named last changes fastest.
Arguments:
- tokens: bfloat16 [64, 256, 768], P('ep', 'sp'), may hold values from -6 to 6
- cotangent: bfloat16 [64, 256, 768], P('ep', 'sp'), may hold values from -6 to 6
- w_query: bfloat16 [768, 768], P(('sp', 'ep')), may hold values from -0.21875 to 0.21875
- w_key: bfloat16 [768, 768], P(('sp', 'ep')), may hold values from -0.21875 to 0.21875
- w_value: bfloat16 [768, 768], P(('sp', 'ep')), may hold values from -0.21875 to 0.21875
- w_output: bfloat16 [768, 768], P(('sp', 'ep')), may hold values from -1.25 to 1.25
- gain_attn: bfloat16 [768], P(('sp', 'ep')), may hold values from 0.25 to 1.75
- gain_ffn: bfloat16 [768], P(('sp', 'ep')), may hold values from 0.25 to 1.75
- router: bfloat16 [768, 64], P(('sp', 'ep')), may hold values from -0.15625 to 0.15625
- bias_table: bfloat16 [384], P(('sp', 'ep')), may hold values from -4 to 4
- w_in: bfloat16 [64, 768, 3072], P('ep', None, 'sp'), may hold values from -0.21875 to 0.21875
- w_out: bfloat16 [64, 3072, 768], P('ep', 'sp'), may hold values from -0.109375 to 0.109375
- routes: int32 [64, 256, 2], P('ep', 'sp'), may hold values from 0 to 63, all different within a row; in each aligned block of 128 rows (0 to 127, 128 to 255, ..., all dimensions but the last counted through in order) at most 6 rows name the same one
- buckets: int32 [256], replicated, may hold values from 0 to 31
Outputs:
- mixed: bfloat16 [64, 256, 768], P('ep', 'sp')
- d_tokens: float32 [64, 256, 768], P('ep', 'sp')
- grad_w_query: float32 [768, 768], P(('sp', 'ep'))
- grad_w_key: float32 [768, 768], P(('sp', 'ep'))
- grad_w_value: float32 [768, 768], P(('sp', 'ep'))
- grad_w_output: float32 [768, 768], P(('sp', 'ep'))
- grad_gain_attn: float32 [768], P(('sp', 'ep'))
- grad_gain_ffn: float32 [768], P(('sp', 'ep'))
- grad_router: float32 [768, 64], P(('sp', 'ep'))
- grad_bias_table: float32 [384], P(('sp', 'ep'))
- grad_w_in: float32 [64, 768, 3072], P('ep', None, 'sp')
- grad_w_out: float32 [64, 3072, 768], P('ep', 'sp')
Inputs may be any that keep to these rules, and one draw needn't show every extreme that they name: `routes`: each row names two different experts; in the rows of one device (aligned blocks of 128 tokens in the order of sequences and positions) no expert is named by more than 6 rows.
All inputs are finite; a program needn't handle non-finite values.
Results may differ from a plain program's by a relative error of at most 0.024.
Values may be sent and summed in bfloat16 or wider, within the bound.
A program may use at most 192 MiB of HBM per device.

v0:
```python
from types import SimpleNamespace

import jax
import jax.numpy as jnp
from jax import lax
from jax.experimental import pallas as pl
from jax.experimental.pallas import tpu as pltpu
from jax.sharding import PartitionSpec as P

D = 768
H = 12
HD = 64
HH = H // 2
HW = HH * HD
EXP = 64
EPS = 1e-06
CAP = 6
SLOT = 8
SLOTS = EXP * SLOT
BIG = 256
SMALL = 128
QROW = 16
QW = 3 * HW
PW = QW + 128
SIDE = 4
STRIDES = (16, 4, 1)
PARTS = ((0, 512, (2, 1, 0)), (512, 384, (0, 2, 1)), (896, 384, (1, 0, 2)))
MESH = pl.DeviceIdType.MESH
ROUTER = QW
GAIN = QW + 64
F32 = jnp.float32
BF16 = jnp.bfloat16
VMEM_LIMIT = 59 * 1024 * 1024


def iota(shape, axis):
    return lax.broadcasted_iota(jnp.int32, shape, axis)


def nn(left, right):
    return lax.dot_general(left, right, (((1,), (0,)), ((), ())), preferred_element_type=F32)


def nt(left, right):
    return lax.dot_general(left, right, (((1,), (1,)), ((), ())), preferred_element_type=F32)


def tn(left, right):
    return lax.dot_general(left, right, (((0,), (0,)), ((), ())), preferred_element_type=F32)


def chunk_entry(rows):
    owner = jnp.right_shift(rows, 4)
    inner = jnp.bitwise_and(rows, 15)
    half = (inner >= 6).astype(jnp.int32)
    inside = inner - 6 * half
    entry = half * (32 * H // 2) + owner * 3 + inside
    return jnp.where((inner < 12) & (inside < 3), entry, -1)


def hot(condition):
    return jnp.where(condition, 1.0, 0.0).astype(BF16)


PLANE = SIDE * SIDE
WIDE = 2 * 6 * PLANE
THICK = PLANE * QROW


def chunk_hot(turned, place):
    axis = 1 if turned else 0
    row = iota((1, WIDE) if turned else (WIDE, 1), axis)
    rows = iota((THICK, WIDE) if turned else (WIDE, THICK), 1 - axis)
    half = (row >= WIDE // 2).astype(jnp.int32)
    row = row - half * (WIDE // 2)
    owner = jnp.right_shift(row * 10923, 16)
    inner = row - owner * 6
    return hot(rows == place(half, owner * QROW, inner))


def projection_row(half, start, inner):
    return start + 6 * half + inner


def output_row(third):
    def place(half, start, inner):
        later = (inner >= 3).astype(jnp.int32)
        return jnp.where(inner - 3 * later == third, start + 12 + 2 * later + half, -1)

    return place


def rms_of(values):
    return lax.rsqrt(jnp.mean(values * values, axis=-1, keepdims=True) + EPS)


def unpack_chunks(v):
    pick = chunk_hot(False, projection_row)
    picks = [chunk_hot(False, output_row(third)) for third in range(3)]
    rows = WIDE // 2
    for x in range(SIDE):
        held = v.pack[x].reshape(THICK, PW)
        own = nn(pick, held).astype(BF16)
        v.full[x * rows : (x + 1) * rows, :] = own[:rows]
        v.full[D // 2 + x * rows : D // 2 + (x + 1) * rows, :] = own[rows:]
        out = sum(nn(picks[third], held[:, third * HW : (third + 1) * HW]) for third in range(3)).astype(BF16)
        v.output[x * rows : (x + 1) * rows, :HW] = out[:rows]
        v.output[x * rows : (x + 1) * rows, HW:] = out[rows:]
    v.gains[...] = v.full[:, QW:].astype(F32).T


def distance_bias(v, bucket_ref, seq):
    entry = chunk_entry(iota((EXP * QROW, 1), 0))
    bucket_of = jnp.right_shift(entry * 5462, 16)
    head_of = entry - bucket_of * H
    column = iota((EXP * QROW, 128), 1)
    tail = v.pack[:, :, :, :, QW:].reshape(EXP * QROW, 128)
    here_now = (entry >= 0) & (head_of == lax.axis_index("sp") * HH + column) & (column < HH)
    table = jnp.where(here_now, tail[:, 66:67].astype(F32), 0.0).astype(BF16)
    bucket_here = jnp.where(entry >= 0, bucket_of, -1)
    by_distance = tn(table, hot(bucket_here == bucket_ref[...]))[0:16, :].astype(BF16)
    turn = hot(jnp.bitwise_and(iota((seq, seq), 0) + iota((seq, seq), 1), seq - 1) == 0)
    v.bias[...] = nn(by_distance, turn)


def attend(v, seq):
    v.qkv[...] = nn(v.normed[...], v.full[:, :QW]).astype(BF16)
    causal = iota((seq, seq), 1) <= iota((seq, seq), 0)
    for head in range(HH):
        at = head * HD
        query = v.qkv[:, at : at + HD]
        key = v.qkv[:, HW + at : HW + at + HD]
        value = v.qkv[:, 2 * HW + at : 2 * HW + at + HD]
        bias = pltpu.roll(jnp.broadcast_to(v.bias[head : head + 1, :], (seq, seq)), 0, 1, stride=1, stride_axis=0)
        scores = jnp.where(causal, nt(query, key) * (HD**-0.5) + bias, -jnp.inf)
        peak = jnp.max(scores, axis=-1, keepdims=True)
        grown = jnp.exp(scores - peak)
        probs = grown / jnp.sum(grown, axis=-1, keepdims=True)
        v.probs[head] = probs
        v.attended[:, at : at + HD] = nn(probs.astype(BF16), value).astype(BF16)


def named_experts(v, count):
    return [(v.table[:, 8 + k : 9 + k].astype(jnp.int32) == iota((count, EXP), 1)).astype(F32) for k in range(2)]


def place_rows(v, routes_ref, count):
    row = iota((128, count), 0)
    routes = jnp.where(row == 0, routes_ref[0:1, :], jnp.where(row == 1, routes_ref[1:2, :], 0)).astype(F32).T
    column = iota((count, 128), 1)
    table = jnp.where(column == 8, routes[:, 0:1], jnp.where(column == 9, routes[:, 1:2], -1.0))
    v.table[...] = table
    named = named_experts(v, count)
    before = hot(iota((count, count), 1) < iota((count, count), 0))
    earlier = nn(before, (named[0] + named[1]).astype(BF16))
    for k in range(2):
        rank = jnp.sum(earlier * named[k], axis=-1, keepdims=True)
        start = routes[:, k : k + 1] * SLOT
        upper = (rank >= 3).astype(F32)
        table = jnp.where(column == 4 * k, start + rank, table)
        for third in range(3):
            value = jnp.where(rank - 3 * upper == third, start + CAP + upper, -1.0)
            table = jnp.where(column == 4 * k + 1 + third, value, table)
    v.table[...] = table


def fill_waves(v, cot_ref, count):
    normed = (v.resid[...] * rms_of(v.resid[...]) * v.gains[65:66, :]).astype(BF16)
    v.ffn[...] = normed
    logits = nn(normed, v.full[:, ROUTER : ROUTER + EXP])
    chosen = [jnp.sum(logits * one, axis=-1, keepdims=True) for one in named_experts(v, count)]
    peak = jnp.maximum(chosen[0], chosen[1])
    grown = [jnp.exp(one - peak) for one in chosen]
    total = grown[0] + grown[1]
    gates = [one / total for one in grown]
    column = iota((count, 128), 1)
    v.gates[...] = jnp.where(column == 0, gates[0], jnp.where(column == 1, gates[1], 0.0))
    upstream = cot_ref[...].astype(F32)
    slots = iota((SLOTS, count), 0)
    turned = v.table[...].T.astype(jnp.int32)
    place = [hot(slots == turned[n : n + 1, :]) for n in range(8)]
    spread = [(gates[k] * upstream).astype(BF16) for k in range(2)]
    either = place[0] + place[4]
    for third in range(3):
        there = slice(third * BIG, (third + 1) * BIG)
        big = nn(either, normed[:, there])
        there_small = slice(third * SMALL, (third + 1) * SMALL)
        small = 0.0
        for k in range(2):
            tail = place[4 * k + 1 + third]
            big = big + nn(tail, spread[k][:, D - BIG :])
            small = small + nn(place[4 * k], spread[k][:, there_small]) + nn(tail, spread[k][:, 3 * SMALL : 4 * SMALL])
        v.big0[:, :, :, :, there] = big.astype(BF16).reshape(SIDE, SIDE, SIDE, SLOT, BIG)
        v.small0[:, :, :, :, there_small] = small.astype(BF16).reshape(SIDE, SIDE, SIDE, SLOT, SMALL)


GROUP = 32
LOAD = GROUP * CAP
HELD = GROUP * SLOT


def unpacking(turned):
    axis = 1 if turned else 0
    row = iota((1, LOAD) if turned else (LOAD, 1), axis)
    slots = iota((HELD, LOAD) if turned else (LOAD, HELD), 1 - axis)
    owner = jnp.right_shift(row * 10923, 16)
    inner = row - owner * CAP
    upper = (inner >= 3).astype(jnp.int32)
    tails = [hot(slots == jnp.where(inner - 3 * upper == third, owner * SLOT + CAP + upper, -1)) for third in range(3)]
    return hot(slots == owner * SLOT + inner), tails


def expert_grad_kernel(turned_ref, drows_ref, act_ref, dpre_ref, gin_ref, gout_ref):
    gin_ref[0] = nn(turned_ref[...], dpre_ref[...])
    gout_ref[0] = nn(act_ref[...], drows_ref[...])


def split_two(values):
    high = values.astype(BF16)
    return high, (values - high.astype(F32)).astype(BF16)


def combine(v, cot_ref, mixed_ref, count):
    resid = v.resid[...]
    upstream = cot_ref[...].astype(F32)
    gates = [v.gates[:, k : k + 1] for k in range(2)]
    table = v.table[...].astype(jnp.int32)
    slots = iota((count, SLOTS), 1)
    place = [hot(slots == table[:, n : n + 1]) for n in range(8)]
    big = v.big_back[...].reshape(SLOTS, 3 * BIG)
    small = v.small_back[...].reshape(SLOTS, 3 * SMALL)
    outs = []
    for k in range(2):
        last, most = 0.0, 0.0
        for third in range(3):
            tail = place[4 * k + 1 + third]
            last = last + nn(tail, small[:, third * SMALL : (third + 1) * SMALL])
            most = most + nn(tail, big[:, third * BIG : (third + 1) * BIG])
        outs.append(jnp.concatenate([nn(place[4 * k], small), last, most], axis=1))
    mixed_ref[0] = (resid + (gates[0] * outs[0] + gates[1] * outs[1])).astype(BF16)
    d_gates = [jnp.sum(one * upstream, axis=-1, keepdims=True) for one in outs]
    inner = gates[0] * d_gates[0] + gates[1] * d_gates[1]
    named = named_experts(v, count)
    d_logits = sum(named[k] * (gates[k] * (d_gates[k] - inner)) for k in range(2)).astype(BF16)
    d_normed = nn(place[0] + place[4], big) + nt(d_logits, v.full[:, ROUTER : ROUTER + EXP])
    rms = rms_of(resid)
    u = d_normed * v.gains[65:66, :]
    v.dresid[...] = upstream + rms * u - resid * (rms * rms * rms) * jnp.mean(u * resid, axis=-1, keepdims=True)
    return d_logits, jnp.sum(d_normed * resid * rms, axis=0, keepdims=True)


def attend_back(v, seq):
    d_attended = nt(v.branch[...].reshape(seq, D), v.output[...]).astype(BF16)
    flip = hot(iota((seq, seq), 0) + iota((seq, seq), 1) == seq - 1)
    v.ddist[...] = jnp.zeros_like(v.ddist)
    for head in range(HH):
        at = head * HD
        query = v.qkv[:, at : at + HD]
        key = v.qkv[:, HW + at : HW + at + HD]
        value = v.qkv[:, 2 * HW + at : 2 * HW + at + HD]
        d_out = d_attended[:, at : at + HD]
        probs = v.probs[head]
        d_probs = nt(d_out, value)
        row_dot = jnp.sum(probs * d_probs, axis=-1, keepdims=True)
        d_scores = (probs * (d_probs - row_dot)).astype(BF16)
        v.dqkv[:, at : at + HD] = (nn(d_scores, key) * (HD**-0.5)).astype(BF16)
        v.dqkv[:, HW + at : HW + at + HD] = (tn(d_scores, query) * (HD**-0.5)).astype(BF16)
        v.dqkv[:, 2 * HW + at : 2 * HW + at + HD] = tn(probs.astype(BF16), d_out).astype(BF16)
        skewed = pltpu.roll(nn(d_scores, flip), 0, 1, stride=1, stride_axis=0)
        v.ddist[head : head + 1, :] = jnp.sum(skewed, axis=0, keepdims=True)


def table_gradient(v, bucket_ref):
    entry = chunk_entry(iota((EXP * QROW, 1), 0))
    bucket_of = jnp.right_shift(entry * 5462, 16)
    pick = hot(jnp.where(entry >= 0, bucket_of, -1) == bucket_ref[...])
    high, low = split_two(pltpu.roll(v.ddist[...], 1, 1))
    by_head = nt(pick, high) + nt(pick, low)
    column = iota(by_head.shape, 1)
    mine = (entry >= 0) & (entry - bucket_of * H == lax.axis_index("sp") * HH + column) & (column < HH)
    return jnp.sum(jnp.where(mine, by_head, 0.0), axis=-1, keepdims=True)


def here():
    owner = lax.axis_index("ep")
    return (owner // 16, owner // 4 % 4, owner % 4)


def across(axis, shift):
    owner, place = lax.axis_index("ep"), here()[axis]
    return {"ep": owner + ((place + shift) % SIDE - place) * STRIDES[axis]}


def other_core():
    return {"sp": 1 - lax.axis_index("sp")}


def greet():
    barrier = pltpu.get_barrier_semaphore()
    pl.semaphore_signal(barrier, inc=1, device_id=other_core(), device_id_type=MESH)
    for axis in range(3):
        for shift in range(1, SIDE):
            pl.semaphore_signal(barrier, inc=1, device_id=across(axis, shift), device_id_type=MESH)


def meet():
    pl.semaphore_wait(pltpu.get_barrier_semaphore(), 1 + 3 * (SIDE - 1))


def remote(source, target, send, receive, device):
    copy = pltpu.make_async_remote_copy(
        src_ref=source, dst_ref=target, send_sem=send, recv_sem=receive, device_id=device, device_id_type=MESH
    )
    copy.start()
    return copy


class Wave:
    ORDERS = ((2, 1, 0), (0, 2, 1), (1, 0, 2))

    def __init__(self, width, buffers, send, recv, local):
        self.width, self.buffers, self.send, self.recv, self.local = width, buffers, send, recv, local
        self.place, self.copies, self.kept = here(), {}, {}

    def block(self, ref, axis, value, third):
        index = tuple(value if other == axis else pl.ds(0, SIDE) for other in range(3))
        return ref.at[index + (slice(None), pl.ds(third * self.width, self.width))]

    def step(self, phase):
        for third, order in enumerate(self.ORDERS):
            if phase:
                self.settle(phase - 1, third)
            axis = order[phase]
            source, target = self.buffers[phase], self.buffers[phase + 1]
            spot = self.place[axis]
            for shift in (2, 1, 3):
                self.copies[phase, third, shift] = remote(
                    self.block(source, axis, (spot + shift) % SIDE, third),
                    self.block(target, axis, spot, third),
                    self.send.at[phase, third, shift - 1],
                    self.recv.at[phase, third, shift - 1],
                    across(axis, shift),
                )
            own = pltpu.make_async_copy(
                self.block(source, axis, spot, third), self.block(target, axis, spot, third), self.local.at[phase, third]
            )
            own.start()
            self.kept[phase, third] = own

    def settle(self, phase, third):
        for shift in range(1, SIDE):
            self.copies[phase, third, shift].wait_recv()
        self.kept[phase, third].wait()

    def land(self):
        for third in range(3):
            self.settle(2, third)

    def push(self, target, send, recv):
        source = self.buffers[3]
        pushes = []
        for third in range(3):
            self.settle(2, third)
            columns = (slice(None),) * 4 + (pl.ds(third * self.width, self.width),)
            pushes.append(remote(source.at[columns], target.at[columns], send.at[third], recv.at[third], other_core()))
        return pushes

    def sent(self):
        for copy in self.copies.values():
            copy.wait_send()


def experts(v):
    rows, act, bend, win, wout, win_turned, wout_turned = v.rows, v.act, v.bend, v.win, v.wout, v.win_turned, v.wout_turned
    drows_ref, dpre_ref = v.drows, v.dpre
    core_send, core_recv = v.push_send, v.push_recv

    def wave(n, width, buffers):
        return Wave(width, buffers, v.wave_send.at[n], v.wave_recv.at[n], v.wave_local.at[n])

    big = wave(0, BIG, (v.big0, v.big1, v.big2, v.big3))
    small = wave(1, SMALL, (v.small0, v.small1, v.small2, v.small3))
    back_small = wave(2, SMALL, (v.rsmall0, v.rsmall1, v.rsmall2, v.small_back))
    back_big = wave(3, BIG, (v.rbig0, v.rbig1, v.rbig2, v.big_back))
    for phase in range(3):
        big.step(phase)
        small.step(phase)
    pushes = big.push(v.big_theirs, core_send.at[0], core_recv.at[0])
    main, tails = unpacking(False)
    main_turned, tails_turned = unpacking(True)
    load = EXP * CAP
    hidden = win.shape[1]
    step = 512

    def groups(half, ref, width):
        packed = ref[...].reshape(SLOTS, 3 * width)
        for group in range(2):
            held = packed[group * HELD : (group + 1) * HELD]
            rest = 0.0
            for third in range(3):
                rest = rest + nn(tails[third], held[:, third * width : (third + 1) * width])
            first = half * load + group * LOAD
            yield slice(first, first + LOAD), nn(main, held).astype(BF16), rest.astype(BF16)

    def forward(half, source):
        there = slice(half * load, (half + 1) * load)
        for where, first, rest in groups(half, source, BIG):
            rows[where, :] = first
            drows_ref[where, D - BIG :] = rest
        normed = rows[there, :]
        for start in range(0, hidden, step):
            columns = slice(start, start + step)
            pre = nn(normed, win[:, columns])
            square = pre * pre
            slope = 0.7978845608028654
            upper = 0.5 + 0.5 * jnp.tanh(pre * (slope + (slope * 0.044715) * square))
            grown = pre * upper
            act[there, columns] = grown.astype(BF16)
            bend[there, columns] = upper + grown * (1.0 - upper) * (2 * slope + (6 * slope * 0.044715) * square)
        return nn(act[there, :], wout[...]).astype(BF16)

    def backward(half, source):
        there = slice(half * load, (half + 1) * load)
        for where, first, rest in groups(half, source, SMALL):
            drows_ref[where, : 3 * SMALL] = first
            drows_ref[where, 3 * SMALL : 4 * SMALL] = rest
        d_rows = drows_ref[there, :]
        for start in range(0, hidden, step):
            columns = slice(start, start + step)
            dpre_ref[there, columns] = (nn(d_rows, wout_turned[:, columns]) * bend[there, columns]).astype(BF16)
        return nn(dpre_ref[there, :], win_turned[...]).astype(BF16)

    def pack(values, last, width):
        for third in range(3):
            for group in range(2):
                there = slice(group * LOAD, (group + 1) * LOAD)
                own = nn(main_turned, values[there, third * width : (third + 1) * width])
                yield third, group, own + nn(tails_turned[third], last[there, :])

    def pack_small(out):
        return pack(out, out[:, 3 * SMALL : 4 * SMALL], SMALL)

    def pack_big(grad, out):
        return pack(grad, out[:, D - BIG :], BIG)

    def hand_over(packed, outgoing, incoming, n):
        copies = []
        for third, group, values in packed:
            outgoing[third, group * HELD : (group + 1) * HELD] = values.astype(BF16)
            if group:
                copies.append(
                    remote(outgoing.at[third], incoming.at[third], core_send.at[n, third], core_recv.at[n, third], other_core())
                )
        return copies

    def join(packed, incoming, copies, target, width):
        for third, group, values in packed:
            if group == 0:
                copies[third].wait_recv()
            total = (values + incoming[third, group * HELD : (group + 1) * HELD].astype(F32)).astype(BF16)
            target[2 * group : 2 * group + 2, :, :, :, third * width : (third + 1) * width] = total.reshape(
                SIDE // 2, SIDE, SIDE, SLOT, width
            )

    out = forward(0, v.big3)
    for push in pushes:
        push.wait_recv()
    pushes += small.push(v.small_theirs, core_send.at[1], core_recv.at[1])
    out_theirs = forward(1, v.big_theirs)
    small_copies = hand_over(pack_small(out_theirs), v.small_out, v.small_in, 2)
    grad = backward(0, v.small3)
    join(pack_small(out), v.small_in, small_copies, v.rsmall0, SMALL)
    back_small.step(0)
    for push in pushes[3:]:
        push.wait_recv()
    grad_theirs = backward(1, v.small_theirs)
    big_copies = hand_over(pack_big(grad_theirs, out_theirs), v.big_out, v.big_in, 3)
    back_small.step(1)
    join(pack_big(grad, out), v.big_in, big_copies, v.rbig0, BIG)
    back_big.step(0)
    back_small.step(2)
    win[:, :D] = rows[...].T
    back_big.step(1)
    wout[...] = act[...].T
    back_big.step(2)
    for copy in leaving(v):
        copy.start()
    back_small.land()
    back_big.land()
    for copy in pushes + small_copies + big_copies:
        copy.wait_send()
    for one in (big, small, back_small, back_big):
        one.sent()


def load_chunks(v, wq_ref, wk_ref, wv_ref, wo_ref, router_ref, attn_ref, ffn_ref, table_ref):
    v.stage[...] = jnp.zeros_like(v.stage)
    v.out16[...] = jnp.zeros_like(v.out16)
    v.out16[0:6, :] = wo_ref[...]

    def standing(ref):
        size = ref.shape[1]
        values = jnp.broadcast_to(ref[...].astype(F32), (QROW, size))
        kept = jnp.where(iota((QROW, size), 0) == iota((QROW, size), 1), values, 0.0)
        return jnp.sum(kept, axis=1, keepdims=True)

    column = iota((QROW, 64), 1)
    tail = jnp.where(column == 0, standing(attn_ref), 0.0)
    tail = jnp.where(column == 1, standing(ffn_ref), tail)
    tail = jnp.where(column == 2, standing(table_ref), tail).astype(BF16)
    for half in range(2):
        for n, ref in enumerate((wq_ref, wk_ref, wv_ref)):
            v.stage[half, 0:6, n * HW : (n + 1) * HW] = ref[:, half * HW : (half + 1) * HW]
        v.stage[half, 0:6, ROUTER : ROUTER + EXP] = router_ref[...]
        v.stage[half, :, GAIN:] = tail


def own_chunk(v, place):
    sp = lax.axis_index("sp")
    row, col = iota((QROW, QROW), 0), iota((QROW, QROW), 1)
    low = jnp.where((row == col) & (col < 6), 1.0, 0.0)
    high = jnp.where((row == col + 6) & (col < 6), 1.0, 0.0)
    own = jnp.where(sp == 0, low, high).astype(BF16)
    others = jnp.where(sp == 0, high, low).astype(BF16)
    later = (col >= 3).astype(jnp.int32)
    mine = nn(own, v.stage[sp]) + nn(others, v.chunk_got[...])
    v.pack[place[0], place[1], place[2], :, QW:] = mine[:, QW:].astype(BF16)
    for third in range(3):
        there = slice(third * HW, (third + 1) * HW)
        total = mine[:, there]
        for half in range(2):
            pick = hot((col < 6) & (col - 3 * later == third) & (row == 12 + 2 * later + half))
            total = total + nn(pick, v.out16[:, half * HW : (half + 1) * HW])
        v.pack[place[0], place[1], place[2], :, there] = total.astype(BF16)


class Gather:
    def __init__(self, v):
        self.v, self.place, self.copies = v, here(), {}

    def step(self, phase):
        for part, (first, width, order) in enumerate(PARTS):
            index = [pl.ds(0, SIDE) if axis in order[:phase] else self.place[axis] for axis in range(3)]
            block = self.v.pack.at[index[0], index[1], index[2], :, pl.ds(first, width)]
            if phase:
                self.settle(phase - 1, part)
            for shift in (2, 1, 3):
                self.copies[phase, part, shift] = remote(
                    block,
                    block,
                    self.v.gather_send.at[phase, part, shift - 1],
                    self.v.gather_recv.at[phase, part, shift - 1],
                    across(order[phase], shift),
                )

    def settle(self, phase, part):
        for shift in range(1, SIDE):
            self.copies[phase, part, shift].wait_recv()

    def land(self):
        for part in range(3):
            self.settle(2, part)
        for copy in self.copies.values():
            copy.wait_send()


class Reduce:
    def __init__(self, v):
        self.v, self.place, self.copies = v, here(), {}

    def push(self, phase, part, source, target):
        axis = PARTS[part][2][2 - phase]
        for shift in (2, 1, 3):
            self.copies[phase, part, shift] = remote(
                source((self.place[axis] + shift) % SIDE),
                target.at[shift - 1],
                self.v.reduce_send.at[phase, part, shift - 1],
                self.v.reduce_recv.at[phase, part, shift - 1],
                across(axis, shift),
            )

    def added(self, phase, part, own, arrived):
        values = own.astype(F32)
        for shift in range(1, SIDE):
            self.copies[phase, part, shift].wait_recv()
            values = values + arrived[shift - 1].astype(F32)
        return values

    def at(self, axes, axis, value):
        return tuple(value if one == axis else pl.ds(0, SIDE) for one in axes)

    def first(self, part):
        start, width, order = PARTS[part]

        def block(value):
            return self.v.pack.at[self.at((0, 1, 2), order[2], value) + (slice(None), pl.ds(start, width))]

        self.push(0, part, block, self.v.firsts[part])

    def second(self, part):
        start, width, order = PARTS[part]
        own = self.v.pack[self.at((0, 1, 2), order[2], self.place[order[2]]) + (slice(None), pl.ds(start, width))]
        sums = self.v.sums[part]
        sums[...] = self.added(0, part, own, self.v.firsts[part]).astype(BF16)
        self.push(1, part, lambda value: sums.at[self.at(sorted(order[:2]), order[1], value)], self.v.seconds[part])

    def third(self, part):
        order = PARTS[part][2]
        own = self.v.sums[part][self.at(sorted(order[:2]), order[1], self.place[order[1]])]
        pairs = self.v.pairs[part]
        pairs[...] = self.added(1, part, own, self.v.seconds[part]).astype(BF16)
        self.push(2, part, lambda value: pairs.at[value], self.v.thirds[part])

    def total(self, part):
        return self.added(2, part, self.v.pairs[part][self.place[PARTS[part][2][0]]], self.v.thirds[part])


def layer_kernel(names, *refs):
    v = SimpleNamespace(**dict(zip(names, refs, strict=True)))
    for group in ("firsts", "sums", "seconds", "pairs", "thirds"):
        setattr(v, group, [getattr(v, group + str(part)) for part in range(3)])
    greet()
    loads = [pltpu.make_async_copy(v.win_hbm.at[0], v.win, v.load_sem.at[0]), pltpu.make_async_copy(v.wout_hbm.at[0], v.wout, v.load_sem.at[1])]
    for load in loads:
        load.start()
    sp = lax.axis_index("sp")
    place = here()
    count = v.tok.shape[0]
    seq = 2 * count

    def to_core(source, target, n):
        return remote(source, target, v.core_send.at[n], v.core_recv.at[n], other_core())

    load_chunks(v, v.wq, v.wk, v.wv, v.wo, v.router, v.gain_attn, v.gain_ffn, v.bias_table)
    v.seq[sp] = v.tok[...]
    meet()
    chunk_copy = to_core(v.stage.at[1 - sp], v.chunk_got, 0)
    tok_copy = to_core(v.tok, v.seq.at[sp], 1)
    chunk_copy.wait()
    own_chunk(v, place)
    gather = Gather(v)
    gather.step(0)
    place_rows(v, v.routes, count)
    gather.step(1)
    tok_copy.wait()
    inputs = v.seq[...].reshape(seq, D).astype(F32)
    rms = rms_of(inputs)
    gather.step(2)
    for load in loads:
        load.wait()
    v.win_turned[...] = v.win[...].T
    v.wout_turned[...] = v.wout[...].T
    gather.land()
    unpack_chunks(v)
    v.normed[...] = (inputs * rms * v.gains[64:65, :]).astype(BF16)
    distance_bias(v, v.buckets, seq)
    attend(v, seq)
    v.halves[...] = nn(v.attended[...], v.output[...]).reshape(v.halves.shape)
    half_copy = to_core(v.halves.at[1 - sp], v.half_got, 2)
    half_copy.wait()
    v.resid[...] = v.tok[...].astype(F32) + v.halves[sp] + v.half_got[...]
    fill_waves(v, v.cot, count)
    experts(v)
    d_logits, g_ffn = combine(v, v.cot, v.mixed, count)
    v.branch[sp] = v.dresid[...].astype(BF16)
    branch_copy = to_core(v.branch.at[sp], v.branch.at[sp], 3)
    g_router = tn(d_logits, v.ffn[...])
    to_chunk = chunk_hot(True, projection_row)
    to_output = [chunk_hot(True, output_row(third)) for third in range(3)]
    branch_copy.wait()
    attend_back(v, seq)
    d_branch = v.branch[...].reshape(seq, D)
    g_output = tn(v.attended[...], d_branch).astype(BF16)
    reduce = Reduce(v)
    rows = WIDE // 2

    def split(values, x, second):
        return jnp.concatenate([values[x * rows : (x + 1) * rows], second[x * rows : (x + 1) * rows]], axis=0)

    for third in range(3):
        there = slice(third * HW, (third + 1) * HW)
        gradient = tn(v.normed[...], v.dqkv[:, there]).astype(BF16)
        for x in range(SIDE):
            total = nn(to_chunk, split(gradient[: D // 2], x, gradient[D // 2 :]))
            total = total + nn(to_output[third], split(g_output[:, :HW], x, g_output[:, HW:]))
            v.pack[x, :, :, :, there] = total.astype(BF16).reshape(SIDE, SIDE, QROW, HW)
        if third:
            reduce.first(third - 1)
    d_normed = nt(v.dqkv[...], v.full[:, :QW])
    v.halves[...] = d_normed.reshape(v.halves.shape)
    norm_copy = to_core(v.halves.at[1 - sp], v.norm_got, 4)
    inputs = v.seq[...].reshape(seq, D).astype(F32)
    g_attn = jnp.sum(d_normed * inputs * rms_of(inputs), axis=0, keepdims=True)
    row = iota((64, D), 0)
    tail = jnp.zeros((64, D), F32)
    for n, values in enumerate((*split_two(g_attn), *split_two(g_ffn))):
        tail = jnp.where(row == n, values.astype(F32), tail)
    tail = jnp.concatenate([g_router, tail], axis=0).T.astype(BF16)
    high, low = split_two(table_gradient(v, v.buckets))
    column = iota((THICK, 128), 1)
    for x in range(SIDE):
        there = slice(x * THICK, (x + 1) * THICK)
        total = nn(to_chunk, split(tail[: D // 2], x, tail[D // 2 :]))
        total = jnp.where(column == 68, high[there].astype(F32), jnp.where(column == 69, low[there].astype(F32), total))
        v.pack[x, :, :, :, QW:] = total.astype(BF16).reshape(SIDE, SIDE, QROW, 128)
    reduce.first(2)
    norm_copy.wait()
    inputs = v.tok[...].astype(F32)
    d_normed = v.halves[sp] + v.norm_got[...]
    rms = rms_of(inputs)
    u = d_normed * v.gains[64:65, :]
    drop = inputs * (rms * rms * rms) * jnp.mean(u * inputs, axis=-1, keepdims=True)
    v.dtok[0] = v.dresid[...] + rms * u - drop
    for part in range(3):
        reduce.second(part)
    for part in range(3):
        reduce.third(part)
    for part, (first, width, _) in enumerate(PARTS):
        v.total[:, first : first + width] = reduce.total(part)
    total_copy = to_core(v.total, v.theirs, 5)
    for copy in reduce.copies.values():
        copy.wait_send()
    total_copy.wait()
    for copy in leaving(v):
        copy.wait()


def leaving(v):
    pairs = ((v.win.at[:, pl.ds(0, D)], v.turned_hbm), (v.drows, v.drows_hbm), (v.wout, v.act_hbm), (v.dpre, v.dpre_hbm))
    return [pltpu.make_async_copy(source, target, v.leave_sem.at[n]) for n, (source, target) in enumerate(pairs)]


def end_kernel(total, theirs, dtok_ref, mixed_ref, q_ref, k_ref, v_ref, o_ref, router_ref, attn_ref, ffn_ref, table_ref, dtok_out, mixed_out):
    sp = lax.axis_index("sp")
    dtok_out[...] = dtok_ref[...]
    mixed_out[...] = mixed_ref[...]
    for row in range(6):
        for half in range(2):
            there = 12 + row // 3 * 2 + half
            third = row % 3 * HW
            o_ref[row : row + 1, half * HW : (half + 1) * HW] = total[there : there + 1, third : third + HW]
    mine = jnp.where(sp == 0, total[0:6, :], total[6:12, :])
    other = jnp.where(sp == 0, theirs[0:6, :], theirs[6:12, :])
    for n, ref in enumerate((q_ref, k_ref, v_ref)):
        there = slice(n * HW, (n + 1) * HW)
        ref[:, :HW] = jnp.where(sp == 0, mine[:, there], other[:, there])
        ref[:, HW:] = jnp.where(sp == 0, other[:, there], mine[:, there])
    router_ref[...] = mine[:, ROUTER : ROUTER + EXP] + other[:, ROUTER : ROUTER + EXP]
    extra = mine[:, GAIN:] + other[:, GAIN:]
    diagonal = iota((6, 6), 0) == iota((6, 6), 1)
    for n, ref in enumerate((attn_ref, ffn_ref, table_ref)):
        column = extra[:, 2 * n : 2 * n + 1] + extra[:, 2 * n + 1 : 2 * n + 2]
        ref[...] = jnp.sum(jnp.where(diagonal, column, 0.0), axis=0, keepdims=True)[:, : ref.shape[1]]


def layer_buffers(count, hidden, load):
    seq = 2 * count
    cube = (SIDE, SIDE, SIDE)
    bigs, smalls = (*cube, SLOT, 3 * BIG), (*cube, SLOT, 3 * SMALL)
    buffers = {
        "stage": ((2, QROW, PW), BF16),
        "chunk_got": ((QROW, PW), BF16),
        "out16": ((QROW, D), BF16),
        "pack": ((*cube, QROW, PW), BF16),
        "seq": ((2, count, D), BF16),
        "full": ((D, PW), BF16),
        "output": ((HW, D), BF16),
        "gains": ((128, D), F32),
        "normed": ((seq, D), BF16),
        "bias": ((16, seq), F32),
        "qkv": ((seq, QW), BF16),
        "probs": ((HH, seq, seq), F32),
        "attended": ((seq, HW), BF16),
        "halves": ((2, count, D), F32),
        "half_got": ((count, D), F32),
        "norm_got": ((count, D), F32),
        "resid": ((count, D), F32),
        "dresid": ((count, D), F32),
        "ffn": ((count, D), BF16),
        "table": ((count, 128), F32),
        "gates": ((count, 128), F32),
        "branch": ((2, count, D), BF16),
        "dqkv": ((seq, QW), BF16),
        "ddist": ((16, seq), F32),
        "rows": ((load, D), BF16),
        "drows": ((load, D), BF16),
        "act": ((load, hidden), BF16),
        "dpre": ((load, hidden), BF16),
        "bend": ((load, hidden), F32),
        "win": ((D, hidden), BF16),
        "wout": ((hidden, D), BF16),
        "win_turned": ((hidden, D), BF16),
        "wout_turned": ((D, hidden), BF16),
        "big_out": ((3, SLOTS, BIG), BF16),
        "big_in": ((3, SLOTS, BIG), BF16),
        "small_out": ((3, SLOTS, SMALL), BF16),
        "small_in": ((3, SLOTS, SMALL), BF16),
    }
    for name in ("big0", "big1", "big2", "big3", "big_theirs", "rbig0", "rbig1", "rbig2", "big_back"):
        buffers[name] = (bigs, BF16)
    for name in ("small0", "small1", "small2", "small3", "small_theirs", "rsmall0", "rsmall1", "rsmall2", "small_back"):
        buffers[name] = (smalls, BF16)
    for part, (_, width, _) in enumerate(PARTS):
        buffers[f"firsts{part}"] = ((SIDE - 1, SIDE, SIDE, QROW, width), BF16)
        buffers[f"sums{part}"] = ((SIDE, SIDE, QROW, width), BF16)
        buffers[f"seconds{part}"] = ((SIDE - 1, SIDE, QROW, width), BF16)
        buffers[f"pairs{part}"] = ((SIDE, QROW, width), BF16)
        buffers[f"thirds{part}"] = ((SIDE - 1, QROW, width), BF16)
    semaphores = {
        "load_sem": (2,),
        "leave_sem": (4,),
        "core_send": (6,),
        "core_recv": (6,),
        "gather_send": (3, 3, SIDE - 1),
        "gather_recv": (3, 3, SIDE - 1),
        "reduce_send": (3, 3, SIDE - 1),
        "reduce_recv": (3, 3, SIDE - 1),
        "push_send": (4, 3),
        "push_recv": (4, 3),
        "wave_send": (4, 3, 3, SIDE - 1),
        "wave_recv": (4, 3, 3, SIDE - 1),
        "wave_local": (4, 3, 3),
    }
    scratch = {name: pltpu.VMEM(*one) for name, one in buffers.items()}
    return scratch | {name: pltpu.SemaphoreType.DMA(one) for name, one in semaphores.items()}


def shards(tokens, cotangent, w_query, w_key, w_value, w_output, gain_attn, gain_ffn, router, bias_table, w_in, w_out, routes, buckets):
    count = tokens.shape[1]
    load = 2 * EXP * CAP
    hidden = w_in.shape[2]
    in_vmem = pl.BlockSpec(memory_space=pltpu.VMEM)
    anywhere = pl.BlockSpec(memory_space=pl.ANY)
    given = {
        "wq": w_query,
        "wk": w_key,
        "wv": w_value,
        "wo": w_output,
        "router": router,
        "gain_attn": gain_attn[None],
        "gain_ffn": gain_ffn[None],
        "bias_table": bias_table[None],
        "tok": tokens[0],
        "cot": cotangent[0],
        "routes": routes[0].T,
        "buckets": buckets[None],
        "win_hbm": w_in,
        "wout_hbm": w_out,
    }
    made = {
        "turned_hbm": ((D, load), BF16),
        "drows_hbm": ((load, D), BF16),
        "act_hbm": ((hidden, load), BF16),
        "dpre_hbm": ((load, hidden), BF16),
        "total": ((QROW, PW), F32),
        "theirs": ((QROW, PW), F32),
        "dtok": ((1, count, D), F32),
        "mixed": ((1, count, D), BF16),
    }
    scratch = layer_buffers(count, hidden, load)
    names = [*given, *made, *scratch]
    turned, d_rows, act, d_pre, total, theirs, d_tokens, mixed = pl.pallas_call(
        lambda *refs: layer_kernel(names, *refs),
        in_specs=[anywhere if name.endswith("_hbm") else in_vmem for name in given],
        out_specs=[anywhere if name.endswith("_hbm") else in_vmem for name in made],
        out_shape=[jax.ShapeDtypeStruct(*one) for one in made.values()],
        scratch_shapes=list(scratch.values()),
        compiler_params=pltpu.CompilerParams(vmem_limit_bytes=VMEM_LIMIT, collective_id=0, has_side_effects=True),
        cost_estimate=pl.CostEstimate(flops=20 * 10**9, bytes_accessed=20 * 10**6, transcendentals=load * hidden),
    )(*given.values())

    step = 256
    grad_w_in, grad_w_out = pl.pallas_call(
        expert_grad_kernel,
        grid=(hidden // step,),
        in_specs=[
            pl.BlockSpec((D, load), lambda f: (0, 0)),
            pl.BlockSpec((load, D), lambda f: (0, 0)),
            pl.BlockSpec((step, load), lambda f: (f, 0)),
            pl.BlockSpec((load, step), lambda f: (0, f)),
        ],
        out_specs=[
            pl.BlockSpec((1, D, step), lambda f: (0, 0, f)),
            pl.BlockSpec((1, step, D), lambda f: (0, f, 0)),
        ],
        out_shape=[
            jax.ShapeDtypeStruct((1, D, hidden), F32),
            jax.ShapeDtypeStruct((1, hidden, D), F32),
        ],
        compiler_params=pltpu.CompilerParams(vmem_limit_bytes=VMEM_LIMIT),
        cost_estimate=pl.CostEstimate(flops=4 * load * D * hidden, bytes_accessed=20 * 10**6, transcendentals=0),
    )(turned, d_rows, act, d_pre)

    g_query, g_key, g_value, g_output, g_router, g_attn, g_ffn, g_table, d_tokens, mixed = pl.pallas_call(
        end_kernel,
        out_shape=[jax.ShapeDtypeStruct((6, D), F32)] * 4
        + [jax.ShapeDtypeStruct(shape, F32) for shape in ((6, EXP), (1, 6), (1, 6), (1, 3), (1, count, D))]
        + [jax.ShapeDtypeStruct((1, count, D), BF16)],
        compiler_params=pltpu.CompilerParams(vmem_limit_bytes=VMEM_LIMIT),
        cost_estimate=pl.CostEstimate(flops=10**5, bytes_accessed=2 * 10**6, transcendentals=0),
    )(total, theirs, d_tokens, mixed)
    return (mixed, d_tokens, g_query, g_key, g_value, g_output, g_attn[0], g_ffn[0], g_router, g_table[0], grad_w_in, grad_w_out)


def solution(mesh):
    wide = P(("sp", "ep"), None)
    flat = P(("sp", "ep"))
    rows = P("ep", "sp", None)
    return jax.shard_map(
        shards,
        mesh=mesh,
        in_specs=(rows, rows, wide, wide, wide, wide, flat, flat, wide, flat, P("ep", None, "sp"), rows, rows, P()),
        out_specs=(rows, rows, wide, wide, wide, wide, flat, flat, wide, flat, P("ep", None, "sp"), rows),
        check_vma=False,
    )
```

profile of v0, /device:TPU:1, one launch (start us, length us, event | category | flops | bytes accessed | tf_op | source)
XLA Modules:
  0.0 134.5 jit_solution(3608304656777665431)
XLA Ops:
  0.6 122.1 %shard_map.229 = (bf16[768,768]{1,0:T(8,128)(2,1)}, bf16[768,768]{1,0:T(8,128)(2,1)}, bf16[1536,768]{1,0:T(8,128)(2,1)}, bf16[768,1536]{1,0:T(8,128)(2,1)}, f32[...) custom-call(bf16[6,768]{1,0:T(8,128)(2,1)} %refs_0_.1, ...), custom_call_target="tpu_custom_call" | custom-call | flops 20000000000 | bytes 20000000 | tf_op jit(solution)/shard_map/pallas_call | solution.py:862
  122.8 2.1 %shard_map.230 = (f32[6,768]{1,0:T(8,128)}, f32[6,768]{1,0:T(8,128)}, f32[6,768]{1,0:T(8,128)}, f32[6,768]{1,0:T(8,128)}, f32[6,64]{1,0:T(8,128)}, /*index=5*/f3...) custom-call(f32[16,1280]{1,0:T(8,128)} %get-tuple-element.32.total, ...), custom_call_target="tpu_custom_call" | custom-call | flops 100000 | bytes 2000000 | tf_op jit(solution)/shard_map/pallas_call | solution.py:894
  124.9 9.7 %shard_map.231 = (f32[1,768,1536]{2,1,0:T(8,128)}, f32[1,1536,768]{2,1,0:T(8,128)}) custom-call(bf16[768,768]{1,0:T(8,128)(2,1)} %get-tuple-element.46.turned_ref, bf16[768,768]{1,0:T(8,128)(2,1)} %get-tuple-element.47.drows_ref, bf16[1536,768]{1,0:T(8,128)(2,1)} %get-tuple-element.48.act_ref, bf16[768,1536]{1,0:T(8,128)(2,1)} %get-tuple-element.49.dpre_ref), custom_call_target="tpu_custom_call" | custom-call | flops 3623878656 | bytes 20000000 | tf_op jit(solution)/shard_map/pallas_call | solution.py:873
where the time goes:
time: 135 us
  Pallas kernels  134 us (99%)
    pallas_call x1, Pallas kernels, shards(): pl.pallas_call(lambda *refs: layer_kernel(names, *refs), in_specs=[anywhe...  122 us
    pallas_call x1, Pallas kernels, shards(): pl.pallas_call(expert_grad_kernel, grid=(hidden // step,), in_specs=[pl.B...  9.65 us

commit v1 on v0

--- a/solution.py
+++ b/solution.py
@@ -24,7 +24,7 @@
 PW = QW + 128
 SIDE = 4
 STRIDES = (16, 4, 1)
-PARTS = ((0, 512, (2, 1, 0)), (512, 384, (0, 2, 1)), (896, 384, (1, 0, 2)))
+PARTS = ((0, HW, (2, 1, 0)), (HW, HW, (0, 2, 1)), (2 * HW, HW, (1, 0, 2)), (QW, 128, (2, 1, 0)))
 MESH = pl.DeviceIdType.MESH
 ROUTER = QW
 GAIN = QW + 64
@@ -99,13 +99,22 @@
     picks = [chunk_hot(False, output_row(third)) for third in range(3)]
     rows = WIDE // 2
     for x in range(SIDE):
-        held = v.pack[x].reshape(THICK, PW)
+        held = v.pack[x, :, :, :, :QW].reshape(THICK, QW)
         own = nn(pick, held).astype(BF16)
-        v.full[x * rows : (x + 1) * rows, :] = own[:rows]
-        v.full[D // 2 + x * rows : D // 2 + (x + 1) * rows, :] = own[rows:]
+        v.full[x * rows : (x + 1) * rows, :QW] = own[:rows]
+        v.full[D // 2 + x * rows : D // 2 + (x + 1) * rows, :QW] = own[rows:]
         out = sum(nn(picks[third], held[:, third * HW : (third + 1) * HW]) for third in range(3)).astype(BF16)
         v.output[x * rows : (x + 1) * rows, :HW] = out[:rows]
         v.output[x * rows : (x + 1) * rows, HW:] = out[rows:]
+
+
+def unpack_rest(v):
+    pick = chunk_hot(False, projection_row)
+    rows = WIDE // 2
+    for x in range(SIDE):
+        own = nn(pick, v.pack[x, :, :, :, QW:].reshape(THICK, 128)).astype(BF16)
+        v.full[x * rows : (x + 1) * rows, QW:] = own[:rows]
+        v.full[D // 2 + x * rows : D // 2 + (x + 1) * rows, QW:] = own[rows:]
     v.gains[...] = v.full[:, QW:].astype(F32).T
 
 
@@ -164,7 +173,7 @@
     v.table[...] = table
 
 
-def fill_waves(v, cot_ref, count):
+def fill_waves(v, cot_ref, count, place):
     normed = (v.resid[...] * rms_of(v.resid[...]) * v.gains[65:66, :]).astype(BF16)
     v.ffn[...] = normed
     logits = nn(normed, v.full[:, ROUTER : ROUTER + EXP])
@@ -176,9 +185,6 @@
     column = iota((count, 128), 1)
     v.gates[...] = jnp.where(column == 0, gates[0], jnp.where(column == 1, gates[1], 0.0))
     upstream = cot_ref[...].astype(F32)
-    slots = iota((SLOTS, count), 0)
-    turned = v.table[...].T.astype(jnp.int32)
-    place = [hot(slots == turned[n : n + 1, :]) for n in range(8)]
     spread = [(gates[k] * upstream).astype(BF16) for k in range(2)]
     either = place[0] + place[4]
     for third in range(3):
@@ -208,11 +214,6 @@
     upper = (inner >= 3).astype(jnp.int32)
     tails = [hot(slots == jnp.where(inner - 3 * upper == third, owner * SLOT + CAP + upper, -1)) for third in range(3)]
     return hot(slots == owner * SLOT + inner), tails
-
-
-def expert_grad_kernel(turned_ref, drows_ref, act_ref, dpre_ref, gin_ref, gout_ref):
-    gin_ref[0] = nn(turned_ref[...], dpre_ref[...])
-    gout_ref[0] = nn(act_ref[...], drows_ref[...])
 
 
 def split_two(values):
@@ -265,7 +266,7 @@
         d_scores = (probs * (d_probs - row_dot)).astype(BF16)
         v.dqkv[:, at : at + HD] = (nn(d_scores, key) * (HD**-0.5)).astype(BF16)
         v.dqkv[:, HW + at : HW + at + HD] = (tn(d_scores, query) * (HD**-0.5)).astype(BF16)
-        v.dqkv[:, 2 * HW + at : 2 * HW + at + HD] = tn(probs.astype(BF16), d_out).astype(BF16)
+        v.dqkv[:, 2 * HW + at : 2 * HW + at + HD] = nn(v.probs_turned[head], d_out).astype(BF16)
         skewed = pltpu.roll(nn(d_scores, flip), 0, 1, stride=1, stride_axis=0)
         v.ddist[head : head + 1, :] = jnp.sum(skewed, axis=0, keepdims=True)
 
@@ -385,6 +386,10 @@
     for phase in range(3):
         big.step(phase)
         small.step(phase)
+    v.normed_turned[...] = v.normed[...].T
+    v.attended_turned[...] = v.attended[...].T
+    for head in range(HH):
+        v.probs_turned[head] = v.probs[head].astype(BF16).T
     pushes = big.push(v.big_theirs, core_send.at[0], core_recv.at[0])
     main, tails = unpacking(False)
     main_turned, tails_turned = unpacking(True)
@@ -468,13 +473,13 @@
     pushes += small.push(v.small_theirs, core_send.at[1], core_recv.at[1])
     out_theirs = forward(1, v.big_theirs)
     small_copies = hand_over(pack_small(out_theirs), v.small_out, v.small_in, 2)
-    grad = backward(0, v.small3)
-    join(pack_small(out), v.small_in, small_copies, v.rsmall0, SMALL)
-    back_small.step(0)
     for push in pushes[3:]:
         push.wait_recv()
     grad_theirs = backward(1, v.small_theirs)
     big_copies = hand_over(pack_big(grad_theirs, out_theirs), v.big_out, v.big_in, 3)
+    join(pack_small(out), v.small_in, small_copies, v.rsmall0, SMALL)
+    back_small.step(0)
+    grad = backward(0, v.small3)
     back_small.step(1)
     join(pack_big(grad, out), v.big_in, big_copies, v.rbig0, BIG)
     back_big.step(0)
@@ -557,9 +562,11 @@
         for shift in range(1, SIDE):
             self.copies[phase, part, shift].wait_recv()
 
-    def land(self):
-        for part in range(3):
+    def land(self, parts):
+        for part in parts:
             self.settle(2, part)
+
+    def sent(self):
         for copy in self.copies.values():
             copy.wait_send()
 
@@ -618,7 +625,7 @@
 def layer_kernel(names, *refs):
     v = SimpleNamespace(**dict(zip(names, refs, strict=True)))
     for group in ("firsts", "sums", "seconds", "pairs", "thirds"):
-        setattr(v, group, [getattr(v, group + str(part)) for part in range(3)])
+        setattr(v, group, [getattr(v, group + str(part)) for part in range(4)])
     greet()
     loads = [pltpu.make_async_copy(v.win_hbm.at[0], v.win, v.load_sem.at[0]), pltpu.make_async_copy(v.wout_hbm.at[0], v.wout, v.load_sem.at[1])]
     for load in loads:
@@ -650,16 +657,22 @@
         load.wait()
     v.win_turned[...] = v.win[...].T
     v.wout_turned[...] = v.wout[...].T
-    gather.land()
+    gather.land(range(3))
     unpack_chunks(v)
+    gather.land(range(3, 4))
+    unpack_rest(v)
+    gather.sent()
     v.normed[...] = (inputs * rms * v.gains[64:65, :]).astype(BF16)
     distance_bias(v, v.buckets, seq)
     attend(v, seq)
     v.halves[...] = nn(v.attended[...], v.output[...]).reshape(v.halves.shape)
     half_copy = to_core(v.halves.at[1 - sp], v.half_got, 2)
+    slots = iota((SLOTS, count), 0)
+    turned = v.table[...].T.astype(jnp.int32)
+    slot_hots = [hot(slots == turned[n : n + 1, :]) for n in range(8)]
     half_copy.wait()
     v.resid[...] = v.tok[...].astype(F32) + v.halves[sp] + v.half_got[...]
-    fill_waves(v, v.cot, count)
+    fill_waves(v, v.cot, count, slot_hots)
     experts(v)
     d_logits, g_ffn = combine(v, v.cot, v.mixed, count)
     v.branch[sp] = v.dresid[...].astype(BF16)
@@ -670,7 +683,7 @@
     branch_copy.wait()
     attend_back(v, seq)
     d_branch = v.branch[...].reshape(seq, D)
-    g_output = tn(v.attended[...], d_branch).astype(BF16)
+    g_output = nn(v.attended_turned[...], d_branch).astype(BF16)
     reduce = Reduce(v)
     rows = WIDE // 2
 
@@ -679,13 +692,12 @@
 
     for third in range(3):
         there = slice(third * HW, (third + 1) * HW)
-        gradient = tn(v.normed[...], v.dqkv[:, there]).astype(BF16)
+        gradient = nn(v.normed_turned[...], v.dqkv[:, there]).astype(BF16)
         for x in range(SIDE):
             total = nn(to_chunk, split(gradient[: D // 2], x, gradient[D // 2 :]))
             total = total + nn(to_output[third], split(g_output[:, :HW], x, g_output[:, HW:]))
             v.pack[x, :, :, :, there] = total.astype(BF16).reshape(SIDE, SIDE, QROW, HW)
-        if third:
-            reduce.first(third - 1)
+        reduce.first(third)
     d_normed = nt(v.dqkv[...], v.full[:, :QW])
     v.halves[...] = d_normed.reshape(v.halves.shape)
     norm_copy = to_core(v.halves.at[1 - sp], v.norm_got, 4)
@@ -703,7 +715,7 @@
         total = nn(to_chunk, split(tail[: D // 2], x, tail[D // 2 :]))
         total = jnp.where(column == 68, high[there].astype(F32), jnp.where(column == 69, low[there].astype(F32), total))
         v.pack[x, :, :, :, QW:] = total.astype(BF16).reshape(SIDE, SIDE, QROW, 128)
-    reduce.first(2)
+    reduce.first(3)
     norm_copy.wait()
     inputs = v.tok[...].astype(F32)
     d_normed = v.halves[sp] + v.norm_got[...]
@@ -711,9 +723,9 @@
     u = d_normed * v.gains[64:65, :]
     drop = inputs * (rms * rms * rms) * jnp.mean(u * inputs, axis=-1, keepdims=True)
     v.dtok[0] = v.dresid[...] + rms * u - drop
-    for part in range(3):
+    for part in range(4):
         reduce.second(part)
-    for part in range(3):
+    for part in range(4):
         reduce.third(part)
     for part, (first, width, _) in enumerate(PARTS):
         v.total[:, first : first + width] = reduce.total(part)
@@ -730,8 +742,20 @@
     return [pltpu.make_async_copy(source, target, v.leave_sem.at[n]) for n, (source, target) in enumerate(pairs)]
 
 
-def end_kernel(total, theirs, dtok_ref, mixed_ref, q_ref, k_ref, v_ref, o_ref, router_ref, attn_ref, ffn_ref, table_ref, dtok_out, mixed_out):
+def end_kernel(turned_hbm, drows_hbm, act_hbm, dpre_hbm, total, theirs, dtok_ref, mixed_ref, gin_hbm, gout_hbm, dtok_out, mixed_out, q_ref, k_ref, v_ref, o_ref, router_ref, attn_ref, ffn_ref, table_ref, turned, drows, act, dpre, gin, gout, sem):
     sp = lax.axis_index("sp")
+    pieces = 6
+    wide, tall = D // pieces, act.shape[0] // pieces
+
+    def copy(source, target, n):
+        one = pltpu.make_async_copy(source, target, sem.at[n])
+        one.start()
+        return one
+
+    drows_copy = copy(drows_hbm, drows, 0)
+    act_copies = [copy(act_hbm.at[pl.ds(n * tall, tall)], act.at[pl.ds(n * tall, tall)], 1 + n) for n in range(pieces)]
+    rest = [copy(turned_hbm, turned, 7), copy(dpre_hbm, dpre, 8)]
+    leaving_copies = []
     dtok_out[...] = dtok_ref[...]
     mixed_out[...] = mixed_ref[...]
     for row in range(6):
@@ -751,6 +775,20 @@
     for n, ref in enumerate((attn_ref, ffn_ref, table_ref)):
         column = extra[:, 2 * n : 2 * n + 1] + extra[:, 2 * n + 1 : 2 * n + 2]
         ref[...] = jnp.sum(jnp.where(diagonal, column, 0.0), axis=0, keepdims=True)[:, : ref.shape[1]]
+    drows_copy.wait()
+    for n in range(pieces):
+        act_copies[n].wait()
+        there = pl.ds(n * tall, tall)
+        gout[there, :] = nn(act[there, :], drows[...])
+        leaving_copies.append(copy(gout.at[there], gout_hbm.at[0, there], 9 + n))
+    for one in rest:
+        one.wait()
+    for n in range(pieces):
+        there = pl.ds(n * wide, wide)
+        gin[there, :] = nn(turned[there, :], dpre[...])
+        leaving_copies.append(copy(gin.at[there], gin_hbm.at[0, there], 15 + n))
+    for one in leaving_copies:
+        one.wait()
 
 
 def layer_buffers(count, hidden, load):
@@ -771,6 +809,9 @@
         "qkv": ((seq, QW), BF16),
         "probs": ((HH, seq, seq), F32),
         "attended": ((seq, HW), BF16),
+        "normed_turned": ((D, seq), BF16),
+        "attended_turned": ((HW, seq), BF16),
+        "probs_turned": ((HH, seq, seq), BF16),
         "halves": ((2, count, D), F32),
         "half_got": ((count, D), F32),
         "norm_got": ((count, D), F32),
@@ -811,10 +852,10 @@
         "leave_sem": (4,),
         "core_send": (6,),
         "core_recv": (6,),
-        "gather_send": (3, 3, SIDE - 1),
-        "gather_recv": (3, 3, SIDE - 1),
-        "reduce_send": (3, 3, SIDE - 1),
-        "reduce_recv": (3, 3, SIDE - 1),
+        "gather_send": (3, 4, SIDE - 1),
+        "gather_recv": (3, 4, SIDE - 1),
+        "reduce_send": (3, 4, SIDE - 1),
+        "reduce_recv": (3, 4, SIDE - 1),
         "push_send": (4, 3),
         "push_recv": (4, 3),
         "wave_send": (4, 3, 3, SIDE - 1),
@@ -869,36 +910,29 @@
         cost_estimate=pl.CostEstimate(flops=20 * 10**9, bytes_accessed=20 * 10**6, transcendentals=load * hidden),
     )(*given.values())
 
-    step = 256
-    grad_w_in, grad_w_out = pl.pallas_call(
-        expert_grad_kernel,
-        grid=(hidden // step,),
-        in_specs=[
-            pl.BlockSpec((D, load), lambda f: (0, 0)),
-            pl.BlockSpec((load, D), lambda f: (0, 0)),
-            pl.BlockSpec((step, load), lambda f: (f, 0)),
-            pl.BlockSpec((load, step), lambda f: (0, f)),
-        ],
-        out_specs=[
-            pl.BlockSpec((1, D, step), lambda f: (0, 0, f)),
-            pl.BlockSpec((1, step, D), lambda f: (0, f, 0)),
-        ],
+    grad_w_in, grad_w_out, d_tokens, mixed, g_query, g_key, g_value, g_output, g_router, g_attn, g_ffn, g_table = pl.pallas_call(
+        end_kernel,
+        in_specs=[anywhere] * 4 + [in_vmem] * 4,
+        out_specs=[anywhere] * 2 + [in_vmem] * 10,
         out_shape=[
             jax.ShapeDtypeStruct((1, D, hidden), F32),
             jax.ShapeDtypeStruct((1, hidden, D), F32),
+            jax.ShapeDtypeStruct((1, count, D), F32),
+            jax.ShapeDtypeStruct((1, count, D), BF16),
+        ]
+        + [jax.ShapeDtypeStruct(shape, F32) for shape in ((6, D),) * 4 + ((6, EXP), (1, 6), (1, 6), (1, 3))],
+        scratch_shapes=[
+            pltpu.VMEM((D, load), BF16),
+            pltpu.VMEM((load, D), BF16),
+            pltpu.VMEM((hidden, load), BF16),
+            pltpu.VMEM((load, hidden), BF16),
+            pltpu.VMEM((D, hidden), F32),
+            pltpu.VMEM((hidden, D), F32),
+            pltpu.SemaphoreType.DMA((21,)),
         ],
         compiler_params=pltpu.CompilerParams(vmem_limit_bytes=VMEM_LIMIT),
         cost_estimate=pl.CostEstimate(flops=4 * load * D * hidden, bytes_accessed=20 * 10**6, transcendentals=0),
-    )(turned, d_rows, act, d_pre)
-
-    g_query, g_key, g_value, g_output, g_router, g_attn, g_ffn, g_table, d_tokens, mixed = pl.pallas_call(
-        end_kernel,
-        out_shape=[jax.ShapeDtypeStruct((6, D), F32)] * 4
-        + [jax.ShapeDtypeStruct(shape, F32) for shape in ((6, EXP), (1, 6), (1, 6), (1, 3), (1, count, D))]
-        + [jax.ShapeDtypeStruct((1, count, D), BF16)],
-        compiler_params=pltpu.CompilerParams(vmem_limit_bytes=VMEM_LIMIT),
-        cost_estimate=pl.CostEstimate(flops=10**5, bytes_accessed=2 * 10**6, transcendentals=0),
-    )(total, theirs, d_tokens, mixed)
+    )(turned, d_rows, act, d_pre, total, theirs, d_tokens, mixed)
     return (mixed, d_tokens, g_query, g_key, g_value, g_output, g_attn[0], g_ffn[0], g_router, g_table[0], grad_w_in, grad_w_out)
 
 

time: 135 us -> 130 us (0.963)
  Pallas kernels: 134 us -> 129 us
    pallas_call x1, Pallas kernels: 122 us -> 119 us  [shards(): pl.pallas_call(lambda *refs: layer_kernel(names, *refs), in_specs=[anywhe...]
    pallas_call x2 -> x1, Pallas kernels: 11.7 us -> 9.85 us  [shards(): pl.pallas_call(end_kernel, in_specs=[anywhere] * 4 + [in_vmem] * 4, out_s...]
where the time goes in v1:
time: 130 us
  Pallas kernels  129 us (99%)
    pallas_call x1, Pallas kernels, shards(): pl.pallas_call(lambda *refs: layer_kernel(names, *refs), in_specs=[anywhe...  119 us
    pallas_call x1, Pallas kernels, shards(): pl.pallas_call(end_kernel, in_specs=[anywhere] * 4 + [in_vmem] * 4, out_s...  9.85 us

profile of v1, /device:TPU:1, one launch (start us, length us, event | category | flops | bytes accessed | tf_op | source)
XLA Modules:
  0.0 129.9 jit_solution(17052295006813165430)
XLA Ops:
  0.6 119.2 %shard_map.229 = (bf16[768,768]{1,0:T(8,128)(2,1)}, bf16[768,768]{1,0:T(8,128)(2,1)}, bf16[1536,768]{1,0:T(8,128)(2,1)}, bf16[768,1536]{1,0:T(8,128)(2,1)}, f32[...) custom-call(bf16[6,768]{1,0:T(8,128)(2,1)} %refs_0_.1, ...), custom_call_target="tpu_custom_call" | custom-call | flops 20000000000 | bytes 20000000 | tf_op jit(solution)/shard_map/pallas_call | solution.py:903
  119.9 9.9 %shard_map.230 = (f32[1,768,1536]{2,1,0:T(8,128)}, f32[1,1536,768]{2,1,0:T(8,128)}, f32[1,128,768]{2,1,0:T(8,128)}, bf16[1,128,768]{2,1,0:T(8,128)(2,1)}, f32[6,...) custom-call(bf16[768,768]{1,0:T(8,128)(2,1)} %get-tuple-element.32.t, ...), custom_call_target="tpu_custom_call" | custom-call | flops 3623878656 | bytes 20000000 | tf_op jit(solution)/shard_map/pallas_call | solution.py:913
